TPU v7x, 32 devices: a whole 2x2x4 slice. The times are simulated.
32 devices in a mesh: dp: 4 (over y, core), tensor: 8 (over z, x).
Axes of the slice: x: 2, y: 2, z: 4, core: 2. Of those that a mesh axis runs over, the one named last changes fastest.
Arguments:
- tokens: bfloat16 [1408, 4096], P('dp', 'tensor'), may hold values from -6 to 6
- grad_out: bfloat16 [1408, 4096], P('dp', 'tensor'), may hold values from -6 to 6
- routes: float32 [4, 2, 16], P('dp'), may hold values from 0.005 to 0.3
- counts: int32 [4], P('dp'), may hold values from 176 to 352
- up_weight: bfloat16 [16, 4096, 4096], P(None, 'dp', 'tensor'), may hold values from -0.09375 to 0.09375
- down_weight: bfloat16 [16, 4096, 4096], P(None, 'tensor', 'dp'), may hold values from -0.09375 to 0.09375
Outputs:
- input_grad: bfloat16 [1408, 4096], P('dp', 'tensor')
- up_grad: bfloat16 [16, 4096, 4096], P(None, 'dp', 'tensor')
- down_grad: bfloat16 [16, 4096, 4096], P(None, 'tensor', 'dp')
- route_grad: float32 [4, 2, 16], P('dp')
Inputs may be any that keep to these rules, and one draw needn't show every extreme that they name: `counts`: the valid tokens of a data group, at least one whole segment.
All inputs are finite; a program needn't handle non-finite values.
Results may differ from a plain program's by a relative error of at most 0.02.
Values may be sent and summed in bfloat16 or wider, within the bound.
A program may use at most 192 MiB of HBM per device.

v0:
```python
import jax
import jax.numpy as jnp
from jax import lax
from jax.sharding import PartitionSpec as P

gelu_scale = 0.7978845608
gelu_cubic = 0.044715


def gelu_pair(inputs):
    inner = gelu_scale * (inputs + gelu_cubic * inputs * inputs * inputs)
    tangent = jnp.tanh(inner)
    activated = 0.5 * inputs * (1.0 + tangent)
    derivative = 0.5 * (1.0 + tangent) + 0.5 * inputs * (1.0 - tangent * tangent) * gelu_scale * (
        1.0 + 3.0 * gelu_cubic * inputs * inputs
    )
    return (activated, derivative)


def body(tokens, grad_out, routes, counts, up_weight, down_weight):
    group_rows = tokens.shape[0]
    experts = up_weight.shape[0]
    segments = routes.shape[1]
    seg_rows = group_rows // segments
    high = lax.Precision.HIGHEST
    valid = (jnp.arange(group_rows, dtype=jnp.int32) < counts[0])[:, None]
    masked = jnp.where(valid, grad_out, jnp.zeros_like(grad_out))
    full_tokens, full_grads = (
        lax.all_gather(tokens, "tensor", axis=1, tiled=True),
        lax.all_gather(masked, "tensor", axis=1, tiled=True),
    )
    all_routes = lax.all_gather(routes, "dp", axis=0, tiled=True)
    flat_routes = all_routes.reshape(-1, experts)
    local_up = jnp.dot(
        flat_routes, up_weight.reshape(experts, -1).astype(jnp.float32), precision=high
    )
    local_up = local_up.reshape((-1,) + up_weight.shape[1:]).astype(jnp.bfloat16)
    down_turned = jnp.swapaxes(down_weight, 1, 2)
    local_down = jnp.dot(
        flat_routes, down_turned.reshape(experts, -1).astype(jnp.float32), precision=high
    )
    local_down = local_down.reshape((-1,) + down_turned.shape[1:]).astype(jnp.bfloat16)
    merged_up, merged_down = (
        lax.all_to_all(local_up, "dp", split_axis=0, concat_axis=1, tiled=True),
        lax.all_to_all(local_down, "dp", split_axis=0, concat_axis=1, tiled=True),
    )
    down_terms = []
    slopes = []
    for segment in range(segments):
        seg_tokens = full_tokens[segment * seg_rows : (segment + 1) * seg_rows]
        seg_grads = full_grads[segment * seg_rows : (segment + 1) * seg_rows]
        pre = jnp.dot(seg_tokens, merged_up[segment], preferred_element_type=jnp.float32)
        activated, derivative = gelu_pair(pre)
        activated = activated.astype(jnp.bfloat16)
        slopes.append(derivative)
        down_terms.append(
            jnp.einsum(
                "rd,rh->dh", seg_grads, activated, preferred_element_type=jnp.float32
            ).astype(jnp.bfloat16)
        )
    down_stack = jnp.stack(down_terms, axis=0)
    up_terms = []
    hidden_grads = []
    for segment in range(segments):
        seg_tokens = full_tokens[segment * seg_rows : (segment + 1) * seg_rows]
        seg_grads = full_grads[segment * seg_rows : (segment + 1) * seg_rows]
        back = jnp.einsum(
            "rd,dh->rh", seg_grads, merged_down[segment], preferred_element_type=jnp.float32
        )
        hidden_grad = (back * slopes[segment]).astype(jnp.bfloat16)
        hidden_grads.append(hidden_grad)
        up_terms.append(
            jnp.einsum(
                "rd,rh->dh", seg_tokens, hidden_grad, preferred_element_type=jnp.float32
            ).astype(jnp.bfloat16)
        )
    up_stack = jnp.stack(up_terms, axis=0)
    recv_up, recv_down = (
        lax.all_to_all(up_stack, "dp", split_axis=1, concat_axis=0, tiled=True),
        lax.all_to_all(down_stack, "dp", split_axis=1, concat_axis=0, tiled=True),
    )
    partials = [
        jnp.einsum(
            "rh,dh->rd",
            hidden_grads[segment],
            merged_up[segment],
            preferred_element_type=jnp.float32,
        )
        for segment in range(segments)
    ]
    rounded = lax.optimization_barrier(jnp.concatenate(partials, axis=0).astype(jnp.bfloat16))
    summed = lax.psum_scatter(
        rounded.astype(jnp.float32).astype(jnp.bfloat16), "tensor", scatter_dimension=1, tiled=True
    )
    up_grad = jnp.einsum(
        "ke,kdh->edh", flat_routes, recv_up.astype(jnp.float32), precision=high
    ).astype(jnp.bfloat16)
    down_grad = jnp.einsum(
        "ke,kdh->ehd", flat_routes, recv_down.astype(jnp.float32), precision=high
    ).astype(jnp.bfloat16)
    inner_sums = jnp.einsum("kdh,edh->ke", recv_up, up_weight, preferred_element_type=jnp.float32)
    inner_sums = inner_sums + jnp.einsum(
        "kdh,ehd->ke", recv_down, down_weight, preferred_element_type=jnp.float32
    )
    table = inner_sums.reshape(all_routes.shape)
    totals = lax.psum(table, ("dp", "tensor"))
    route_grad = lax.dynamic_slice_in_dim(totals, lax.axis_index("dp"), 1, 0)
    return (summed, up_grad, down_grad, route_grad)


def solution(mesh):
    return jax.shard_map(
        body,
        mesh=mesh,
        in_specs=(
            P("dp", "tensor"),
            P("dp", "tensor"),
            P("dp", None, None),
            P("dp"),
            P(None, "dp", "tensor"),
            P(None, "tensor", "dp"),
        ),
        out_specs=(
            P("dp", "tensor"),
            P(None, "dp", "tensor"),
            P(None, "tensor", "dp"),
            P("dp", None, None),
        ),
        check_vma=False,
    )
```

profile of v0, /device:TPU:0, one launch (start us, length us, event | category | flops | bytes accessed | tf_op | source)
XLA Modules:
  0.0 695.1 jit_solution(2798309859327716128)
XLA Ops:
  7.2 6.3 all_gather.10
  13.4 23.8 %fusion.16 = bf16[8,1024,512]{2,0,1:T(8,128)(2,1)} fusion(f32[8,16,1]{1,0,2:T(8,128)S(1)} %bitcast.123, bf16[2,8,1024,512]{3,2,1,0:T(8,128)(2,1)} %bitcast.126), kind=kOutput, calls=%fused_computation.20 | convolution fusion | flops 809500672 | bytes 25166336 | tf_op jit(solution)/shard_map/dot_general | solution.py:34
  37.3 9.5 %copy.56 = bf16[8,1024,512]{2,1,0:T(8,128)(2,1)} copy(bf16[8,1024,512]{2,0,1:T(8,128)(2,1)} %fusion.16) | data formatting | bytes 16777216 | tf_op jit(solution)/shard_map/convert_element_type | solution.py:37
  46.8 5.6 all-to-all-start.1
  52.5 0.7 all-gather.5.cloned.1.call-update
  53.2 23.8 %copy.81 = bf16[2,8,1024,512]{3,1,2,0:T(8,128)(2,1)} copy(bf16[2,8,1024,512]{2,3,1,0:T(8,128)(2,1)} %bitcast.113) | data formatting | bytes 33554432
  77.0 12.4 %fusion.13 = bf16[8,1024,512]{2,0,1:T(8,128)(2,1)} fusion(f32[8,16,1]{1,0,2:T(8,128)S(1)} %bitcast.124, bf16[2,8,1024,512]{3,1,2,0:T(8,128)(2,1)} %copy.81), kind=kOutput, calls=%fused_computation.19 | convolution fusion | flops 809500672 | bytes 25166336 | tf_op jit(solution)/shard_map/dot_general | solution.py:39
  89.4 9.8 %copy.54 = bf16[8,1024,512]{2,1,0:T(8,128)(2,1)} copy(bf16[8,1024,512]{2,0,1:T(8,128)(2,1)} %fusion.13) | data formatting | bytes 16777216 | tf_op jit(solution)/shard_map/convert_element_type | solution.py:42
  99.2 46.5 %all-to-all-done.1 = bf16[8,1024,512]{2,1,0:T(8,128)(2,1)} async-done(((bf16[8,1024,512]{2,1,0:T(8,128)(2,1)}), bf16[8,1024,512]{2,1,0:T(8,128)(2,1)}, u32[]{:S(2)}, u32[]{:S(2)}) %all-to-all-start.1) | async-done | bytes 8388640 | tf_op jit(solution)/shard_map/all_to_all | solution.py:44
  145.8 5.7 all-to-all-start
  152.2 0.9 broadcast_select_fusion
  153.1 6.2 fusion.94
  159.2 3.5 fusion.41
  162.8 81.8 %all-to-all-done = bf16[8,1024,512]{2,1,0:T(8,128)(2,1)} async-done(((bf16[8,1024,512]{2,1,0:T(8,128)(2,1)}), bf16[8,1024,512]{2,1,0:T(8,128)(2,1)}, u32[]{:S(2)}, u32[]{:S(2)}) %all-to-all-start) | async-done | bytes 8388640 | tf_op jit(solution)/shard_map/all_to_all | solution.py:45
  244.6 5.8 fusion.95
  250.5 3.8 fusion.50
  254.3 1.3 fusion.19
  255.6 0.9 copy-done
  256.5 0.9 fusion.44
  257.4 1.4 copy-done.2
  258.8 1.0 fusion.47
  259.8 3.3 fusion.20
  263.1 6.3 pad_maximum_fusion
  269.5 21.1 %copy.57 = bf16[2,4096,512]{2,0,1:T(2,128)(2,1)} copy(bf16[2,4096,512]{1,2,0:T(8,128)(2,1)} %pad_maximum_fusion) | data formatting | bytes 16777216 | tf_op jit(solution)/shard_map/stack | solution.py:77
  290.5 5.6 all-to-all-start.2
  296.2 2.9 fusion.21
  299.1 3.3 fusion.22
  302.4 6.3 pad_maximum_fusion.1
  308.7 16.4 %copy.61 = bf16[2,4096,512]{2,0,1:T(2,128)(2,1)} copy(bf16[2,4096,512]{2,1,0:T(8,128)(2,1)} %pad_maximum_fusion.1) | data formatting | bytes 16777216 | tf_op jit(solution)/shard_map/stack | solution.py:61
  325.1 64.2 %all-to-all-done.2 = bf16[2,4096,512]{2,0,1:T(2,128)(2,1)} async-done(((bf16[2,4096,512]{2,0,1:T(2,128)(2,1)}), bf16[2,4096,512]{2,0,1:T(2,128)(2,1)}, u32[]{:S(2)}, u32[]{:S(2)}) %all-to-all-start.2) | async-done | bytes 8388640 | tf_op jit(solution)/shard_map/all_to_all | solution.py:79
  389.3 5.6 all-to-all-start.3
  395.2 3.9 convolution_convert_fusion.5
  399.1 1.5 convolution_convert_fusion.4
  400.6 1.8 pad_maximum_fusion.2
  402.4 24.2 %copy.70 = bf16[16,512,1024]{1,0,2:T(8,128)(2,1)} copy(bf16[16,512,1024]{2,1,0:T(8,128)(2,1)} %param.11) | data formatting | bytes 33554432 | tf_op args[5]
  426.5 21.0 %copy.126 = bf16[2,4,1024,512]{3,1,0,2:T(4,128)(2,1)} copy(bf16[2,4,1024,512]{3,0,2,1:T(2,128)(2,1)} %bitcast.23) | data formatting | bytes 16777216 | tf_op jit(solution)/shard_map/all_to_all | solution.py:79
  447.6 9.5 %copy.65 = bf16[4,2,1024,512]{3,2,1,0:T(8,128)(2,1)} copy(bf16[4,2,1024,512]{3,0,1,2:T(4,128)(2,1)} %bitcast.114) | data formatting | bytes 16777216 | tf_op jit(solution)/shard_map/all_to_all | solution.py:79
  457.1 31.0 %all-to-all-done.3 = bf16[2,4096,512]{2,0,1:T(2,128)(2,1)} async-done(((bf16[2,4096,512]{2,0,1:T(2,128)(2,1)}), bf16[2,4096,512]{2,0,1:T(2,128)(2,1)}, u32[]{:S(2)}, u32[]{:S(2)}) %all-to-all-start.3) | async-done | bytes 8388640 | tf_op jit(solution)/shard_map/all_to_all | solution.py:80
  488.1 21.0 %copy.125 = bf16[2,4,1024,512]{3,1,0,2:T(4,128)(2,1)} copy(bf16[2,4,1024,512]{3,0,2,1:T(2,128)(2,1)} %bitcast.31) | data formatting | bytes 16777216 | tf_op jit(solution)/shard_map/all_to_all | solution.py:80
  509.1 9.5 %copy.68 = bf16[4,2,1024,512]{3,2,1,0:T(8,128)(2,1)} copy(bf16[4,2,1024,512]{3,0,1,2:T(4,128)(2,1)} %bitcast.115) | data formatting | bytes 16777216 | tf_op jit(solution)/shard_map/all_to_all | solution.py:80
  518.6 22.7 %fusion = bf16[16,1024,512]{2,0,1:T(8,128)(2,1)S(1)} fusion(f32[4,2,16]{2,1,0:T(2,128)S(1)} %all_gather.10, bf16[2,4,1024,512]{3,0,2,1:T(2,128)(2,1)} %bitcast.23), kind=kOutput, calls=%fused_computation.2 | convolution fusion | flops 813694976 | bytes 25166336 | tf_op jit(solution)/shard_map/ke,kdh->edh/dot_general | solution.py:95
  541.4 20.5 %copy.71 = bf16[16,1024,512]{2,1,0:T(8,128)(2,1)} copy(bf16[16,1024,512]{2,0,1:T(8,128)(2,1)S(1)} %fusion) | data formatting | bytes 33554432
  561.9 25.3 %fusion.1 = bf16[16,512,1024]{1,0,2:T(8,128)(2,1)} fusion(f32[4,2,16]{2,1,0:T(2,128)S(1)} %all_gather.10, bf16[2,4,1024,512]{3,0,2,1:T(2,128)(2,1)} %bitcast.31), kind=kOutput, calls=%fused_computation.3 | convolution fusion | flops 813694976 | bytes 25166336 | tf_op jit(solution)/shard_map/ke,kdh->ehd/dot_general | solution.py:98
  587.2 23.0 %copy.72 = bf16[16,512,1024]{2,1,0:T(8,128)(2,1)} copy(bf16[16,512,1024]{1,0,2:T(8,128)(2,1)} %fusion.1) | data formatting | bytes 33554432
  610.2 25.5 %fusion.53 = f32[8,16]{1,0:T(8,128)S(1)} fusion(bf16[16,1024,512]{2,1,0:T(8,128)(2,1)} %param.10, bf16[8,1024,512]{2,1,0:T(8,128)(2,1)} %bitcast.120), kind=kOutput, calls=%fused_computation.50 | convolution fusion | flops 134217728 | bytes 25166336 | tf_op jit(solution)/shard_map/kdh,edh->ke/dot_general | solution.py:101
  635.7 12.1 %fusion.61 = f32[8,16]{1,0:T(8,128)S(1)} fusion(f32[8,16]{1,0:T(8,128)S(1)} %fusion.53, bf16[16,512,1024]{1,0,2:T(8,128)(2,1)} %copy.70, bf16[8,1024,512]{2,1,0:T(8,128)(2,1)} %bitcast.112), kind=kOutput, calls=%fused_computation.52 | convolution fusion | flops 134217856 | bytes 25166848 | tf_op jit(solution)/shard_map/kdh,ehd->ke/dot_general | solution.py:102
  647.9 39.9 %psum.7 = f32[4,2,16]{2,1,0:T(2,128)S(1)} all-reduce(f32[4,2,16]{2,1,0:T(2,128)S(1)} %bitcast.125), channel_id=1, replica_groups=mesh['dp'=4,'tensor'=8] {'dp','tensor'}, use_global_device_ids=true, to_apply=%region_1.2 | all-reduce | flops 128 | bytes 1024 | tf_op jit(solution)/shard_map/psum | solution.py:106
  687.8 0.6 constant_dynamic-slice_fusion
  (21 shorter events, 0.4 us)
Async XLA Ops:
  46.8 99.0 %all-to-all-start.1 = ((bf16[8,1024,512]{2,1,0:T(8,128)(2,1)}), bf16[8,1024,512]{2,1,0:T(8,128)(2,1)}, u32[]{:S(2)}, u32[]{:S(2)}) async-start(bf16[8,1024,512]{2,1,0:T(8,128)(2,1)} %copy.56), calls=%async_computation.1 | async-start | bytes 16777216 | tf_op jit(solution)/shard_map/all_to_all | solution.py:44
  52.5 106.8 %all-gather.5.cloned.1.call-start = ((), (), s32[]{:S(2)}) async-start(), calls=%async_computation.6 | async-start | bytes 3244032 | tf_op jit(solution)/shard_map/all_gather | solution.py:29
  99.2 53.0 %copy-start.3 = (bf16[352,512]{1,0:T(8,128)(2,1)S(1)}, bf16[352,512]{1,0:T(8,128)(2,1)}, u32[]{:S(2)}) copy-start(bf16[352,512]{1,0:T(8,128)(2,1)} %param.7) | copy-start | bytes 1081348
  145.8 98.9 %all-to-all-start = ((bf16[8,1024,512]{2,1,0:T(8,128)(2,1)}), bf16[8,1024,512]{2,1,0:T(8,128)(2,1)}, u32[]{:S(2)}, u32[]{:S(2)}) async-start(bf16[8,1024,512]{2,1,0:T(8,128)(2,1)} %copy.54), calls=%async_computation | async-start | bytes 16777216 | tf_op jit(solution)/shard_map/all_to_all | solution.py:45
  151.5 99.0 %all-gather.3.cloned.1.call-start = ((), (), s32[]{:S(2)}) async-start(), calls=%async_computation.5 | async-start | bytes 3244032 | tf_op jit(solution)/shard_map/all_gather | solution.py:30
  250.5 3.8 copy-start.4
  254.3 2.2 copy-start
  254.3 3.1 copy-start.5
  255.6 3.2 copy-start.2
  290.5 98.8 %all-to-all-start.2 = ((bf16[2,4096,512]{2,0,1:T(2,128)(2,1)}), bf16[2,4096,512]{2,0,1:T(2,128)(2,1)}, u32[]{:S(2)}, u32[]{:S(2)}) async-start(bf16[2,4096,512]{2,0,1:T(2,128)(2,1)} %copy.57), calls=%async_computation.3 | async-start | bytes 16777216 | tf_op jit(solution)/shard_map/all_to_all | solution.py:79
  296.2 2.9 copy-start.6
  389.3 98.8 %all-to-all-start.3 = ((bf16[2,4096,512]{2,0,1:T(2,128)(2,1)}), bf16[2,4096,512]{2,0,1:T(2,128)(2,1)}, u32[]{:S(2)}, u32[]{:S(2)}) async-start(bf16[2,4096,512]{2,0,1:T(2,128)(2,1)} %copy.61), calls=%async_computation.4 | async-start | bytes 16777216 | tf_op jit(solution)/shard_map/all_to_all | solution.py:80
  395.0 293.4 %reduce-scatter.2.cloned.1.call-start = ((), (), s32[]{:S(2)}) async-start(), calls=%async_computation.7 | async-start | bytes 3244032 | tf_op jit(solution)/shard_map/reduce_scatter | solution.py:92
  395.2 3.9 copy-start.1
Sparse Core Ops, SparseCore 0:
  55.3 62.1 all-gather.4
  154.9 62.0 all-gather.2
  402.5 74.1 reduce-scatter.1
where the time goes:
time: 705 us; the launch traced here: 695 us
  local copies, waits for them, and re-layouts  224 us (32%)
  waiting for transfers between devices  224 us (32%)
  matrix products  147 us (21%)
  blocking collectives  46.2 us (7%)
  starting transfers between devices  22.9 us (3%)
  other arithmetic  15.3 us (2%)
  between operations  14.8 us (2%)
    unnamed x18, local copies, waits for them, and re-layouts  93.7 us
    all_to_all x1, waiting for transfers between devices, body(): lax.all_to_all(local_down, 'dp', split_axis=0, concat_axis=1, tiled=True)  81.8 us
    all_to_all x1, waiting for transfers between devices, body(): lax.all_to_all(up_stack, 'dp', split_axis=1, concat_axis=0, tiled=True)  64.2 us
    all_to_all x1, waiting for transfers between devices, body(): lax.all_to_all(local_up, 'dp', split_axis=0, concat_axis=1, tiled=True)  46.5 us
    psum x1, blocking collectives, body(): totals = lax.psum(table, ('dp', 'tensor'))  39.9 us
    all_to_all x1, waiting for transfers between devices, body(): lax.all_to_all(down_stack, 'dp', split_axis=1, concat_axis=0, tiled=True)  31 us
    all_to_all x2, local copies, waits for them, and re-layouts, body(): lax.all_to_all(up_stack, 'dp', split_axis=1, concat_axis=0, tiled=True)  30.6 us
    all_to_all x2, local copies, waits for them, and re-layouts, body(): lax.all_to_all(down_stack, 'dp', split_axis=1, concat_axis=0, tiled=True)  30.5 us
  transfers between devices with their start and end apart: 7, of which 4 were waited for; matrix products, arithmetic and copies ran while one was open for 45% of the time, Pallas kernels for 0%

commit v1 on v0

v1 whole, which is shorter than its diff:
```python
import jax
import jax.numpy as jnp
from jax import lax
from jax.experimental import pallas as pl
from jax.experimental.pallas import tpu as pltpu
from jax.sharding import PartitionSpec as P

gelu_scale = 0.7978845608
gelu_cubic = 0.044715
sub = 16
params = pltpu.CompilerParams(vmem_limit_bytes=48 * 1024 * 1024)


def gelu_pair(inputs):
    inner = gelu_scale * (inputs + gelu_cubic * inputs * inputs * inputs)
    tangent = jnp.tanh(inner)
    activated = 0.5 * inputs * (1.0 + tangent)
    derivative = 0.5 * (1.0 + tangent) + 0.5 * inputs * (1.0 - tangent * tangent) * gelu_scale * (
        1.0 + 3.0 * gelu_cubic * inputs * inputs
    )
    return (activated, derivative)


def spread(table):
    full = jnp.kron(table, jnp.eye(sub, dtype=jnp.float32))
    high = lax.reduce_precision(full, 8, 7)
    return high.astype(jnp.bfloat16), (full - high).astype(jnp.bfloat16)


def merge_kernel(mix_ref, weight_ref, out_ref):
    experts, rows, cols = weight_ref.shape
    count = out_ref.shape[0]
    for part in range(rows // sub):
        span = slice(part * sub, (part + 1) * sub)
        block = weight_ref[:, span, :].reshape(experts * sub, cols)
        both = jnp.dot(mix_ref[...], block, preferred_element_type=jnp.float32)
        total = both[: count * sub] + both[count * sub :]
        out_ref[:, span, :] = total.reshape(count, sub, cols).astype(jnp.bfloat16)


def merge(mix, weight, count):
    experts, rows, cols = weight.shape
    step = min(rows, 128)
    return pl.pallas_call(
        merge_kernel,
        grid=(rows // step,),
        in_specs=[
            pl.BlockSpec(mix.shape, lambda b: (0, 0)),
            pl.BlockSpec((experts, step, cols), lambda b: (0, b, 0)),
        ],
        out_specs=pl.BlockSpec((count, step, cols), lambda b: (0, b, 0)),
        out_shape=jax.ShapeDtypeStruct((count, rows, cols), jnp.bfloat16),
        compiler_params=params,
        cost_estimate=pl.CostEstimate(
            flops=4 * count * sub * experts * rows * cols,
            bytes_accessed=2 * (experts + count) * rows * cols,
            transcendentals=0,
        ),
        name="merge",
    )(mix, weight)


def partial_kernel(turned, act_ref, weight_ref, out_ref, total_ref):
    part = pl.program_id(1)
    dims = (((1,), (1,)), ((), ())) if turned else (((1,), (0,)), ((), ()))
    term = lax.dot_general(act_ref[...], weight_ref[...], dims, preferred_element_type=jnp.float32)

    @pl.when(part == 0)
    def _():
        total_ref[...] = term

    @pl.when(part > 0)
    def _():
        total_ref[...] += term

    @pl.when(part == pl.num_programs(1) - 1)
    def _():
        out_ref[...] = total_ref[...].astype(out_ref.dtype)


def partial_product(acts, weight, turned):
    groups, parts, segments, rows, width = acts.shape
    count = groups * segments
    hidden = weight.shape[1] if turned else weight.shape[2]
    weight_spec = (
        pl.BlockSpec((None, hidden, width), lambda k, c: (k, 0, c))
        if turned
        else pl.BlockSpec((None, width, hidden), lambda k, c: (k, c, 0))
    )
    return pl.pallas_call(
        lambda *refs: partial_kernel(turned, *refs),
        grid=(count, parts),
        in_specs=[
            pl.BlockSpec(
                (None, None, None, rows, width),
                lambda k, c: (k // segments, c, k % segments, 0, 0),
            ),
            weight_spec,
        ],
        out_specs=pl.BlockSpec((None, rows, hidden), lambda k, c: (k, 0, 0)),
        out_shape=jax.ShapeDtypeStruct((count, rows, hidden), jnp.bfloat16),
        scratch_shapes=[pltpu.VMEM((rows, hidden), jnp.float32)],
        compiler_params=params,
        cost_estimate=pl.CostEstimate(
            flops=2 * count * parts * rows * width * hidden,
            bytes_accessed=2 * weight.size + 2 * acts.size,
            transcendentals=0,
        ),
        name="partial_product",
    )(acts, weight)


def input_kernel(grad_ref, weight_ref, out_ref):
    out_ref[...] = lax.dot_general(
        grad_ref[...], weight_ref[...], (((1,), (1,)), ((), ())),
        preferred_element_type=jnp.float32,
    ).astype(out_ref.dtype)


def input_product(grads, weight, groups, parts, segments):
    count, rows, hidden = grads.shape
    width = weight.shape[1] // parts
    return pl.pallas_call(
        input_kernel,
        grid=(count, parts),
        in_specs=[
            pl.BlockSpec((None, rows, hidden), lambda k, c: (k, 0, 0)),
            pl.BlockSpec((None, width, hidden), lambda k, c: (k, c, 0)),
        ],
        out_specs=pl.BlockSpec(
            (None, None, None, rows, width),
            lambda k, c: (k // segments, c, k % segments, 0, 0),
        ),
        out_shape=jax.ShapeDtypeStruct((groups, parts, segments, rows, width), jnp.bfloat16),
        compiler_params=params,
        cost_estimate=pl.CostEstimate(
            flops=2 * weight.size * rows,
            bytes_accessed=2 * weight.size + 4 * grads.size,
            transcendentals=0,
        ),
        name="input_product",
    )(grads, weight)


def grad_kernel(segments, mix_ref, left_ref, right_ref, weight_ref, out_ref, inner_ref, term_ref):
    experts, rows, cols = weight_ref.shape
    groups, parts, group_rows, width = right_ref.shape
    seg_rows = group_rows // segments
    count = groups * segments

    @pl.when(pl.program_id(0) == 0)
    def _():
        inner_ref[...] = jnp.zeros_like(inner_ref)

    for k in range(count):
        span = slice((k % segments) * seg_rows, (k % segments + 1) * seg_rows)
        left = left_ref[k // segments, span, :]
        for part in range(parts):
            term = lax.dot_general(
                left, right_ref[k // segments, part, span, :], (((0,), (0,)), ((), ())),
                preferred_element_type=jnp.float32,
            )
            term_ref[k, :, part * width : (part + 1) * width] = term.astype(jnp.bfloat16)
    for part in range(rows // sub):
        span = slice(part * sub, (part + 1) * sub)
        terms = term_ref[:, span, :].reshape(count * sub, cols)
        weights = weight_ref[:, span, :].reshape(experts * sub, cols)
        inner_ref[...] += lax.dot_general(
            terms, weights, (((1,), (1,)), ((), ())), preferred_element_type=jnp.float32
        )
        total = jnp.dot(
            mix_ref[...], jnp.concatenate([terms, terms], axis=0),
            preferred_element_type=jnp.float32,
        )
        out_ref[:, span, :] = total.reshape(experts, sub, cols).astype(jnp.bfloat16)


def expert_grads(mix, left, right, weight, segments):
    experts, rows, cols = weight.shape
    groups, pieces, group_rows, left_width = left.shape
    count = groups * segments
    step = 128
    per = left_width // step
    return pl.pallas_call(
        lambda *refs: grad_kernel(segments, *refs),
        grid=(rows // step,),
        in_specs=[
            pl.BlockSpec(mix.shape, lambda b: (0, 0)),
            pl.BlockSpec(
                (groups, None, group_rows, step), lambda b: (0, b // per, 0, b % per)
            ),
            pl.BlockSpec(right.shape, lambda b: (0, 0, 0, 0)),
            pl.BlockSpec((experts, step, cols), lambda b: (0, b, 0)),
        ],
        out_specs=[
            pl.BlockSpec((experts, step, cols), lambda b: (0, b, 0)),
            pl.BlockSpec((count * sub, experts * sub), lambda b: (0, 0)),
        ],
        out_shape=[
            jax.ShapeDtypeStruct(weight.shape, jnp.bfloat16),
            jax.ShapeDtypeStruct((count * sub, experts * sub), jnp.float32),
        ],
        scratch_shapes=[pltpu.VMEM((count, step, cols), jnp.bfloat16)],
        compiler_params=params,
        cost_estimate=pl.CostEstimate(
            flops=2 * rows * cols * groups * group_rows + 6 * count * sub * experts * rows * cols,
            bytes_accessed=4 * weight.size + 2 * left.size + 2 * right.size,
            transcendentals=0,
        ),
        name="expert_grads",
    )(mix, left, right, weight)


def make_body(n_dp, n_tensor):
    parts = n_tensor // n_dp
    both = ("dp", "tensor")
    moves = []
    for i in range(n_dp):
        for a in range(n_dp):
            for b in range(parts):
                moves.append((i * n_tensor + parts * a + b, a * n_tensor + parts * i + b))
    returns = [(target, source) for source, target in moves]

    def body(tokens, grad_out, routes, counts, up_weight, down_weight):
        group_rows, width = tokens.shape
        experts = up_weight.shape[0]
        segments = routes.shape[1]
        seg_rows = group_rows // segments
        hidden = up_weight.shape[2]
        count = n_dp * segments
        valid = (jnp.arange(group_rows, dtype=jnp.int32) < counts[0])[:, None]
        masked = jnp.where(valid, grad_out, jnp.zeros_like(grad_out))
        moved_tokens = lax.ppermute(tokens, both, moves)
        moved_grads = lax.ppermute(masked, both, moves)
        all_tokens = lax.all_gather(moved_tokens, "tensor", axis=0, tiled=False)
        all_grads = lax.all_gather(moved_grads, "tensor", axis=0, tiled=False)
        all_tokens = all_tokens.reshape(n_dp, parts, group_rows, width)
        all_grads = all_grads.reshape(n_dp, parts, group_rows, width)
        split = (n_dp, parts, segments, seg_rows, width)

        all_routes = lax.all_gather(routes, "dp", axis=0, tiled=True)
        flat_routes = all_routes.reshape(-1, experts)
        mix_merge = jnp.concatenate(spread(flat_routes), axis=0)
        mix_grads = jnp.concatenate(spread(flat_routes.T), axis=1)
        merged_up = merge(mix_merge, up_weight, count)
        merged_down = merge(mix_merge, down_weight, count)

        pre_parts = partial_product(all_tokens.reshape(split), merged_up, False)
        pre_parts = lax.all_to_all(
            pre_parts.reshape(n_dp, group_rows, hidden), "dp", 0, 0, tiled=True
        )
        back_parts = partial_product(all_grads.reshape(split), merged_down, True)
        back_parts = lax.all_to_all(
            back_parts.reshape(n_dp, group_rows, hidden), "dp", 0, 0, tiled=True
        )
        pre = jnp.sum(pre_parts.astype(jnp.float32), axis=0)
        back = jnp.sum(back_parts.astype(jnp.float32), axis=0)
        activated, slope = gelu_pair(pre)
        hidden_grad = (back * slope).astype(jnp.bfloat16)
        all_act = lax.all_gather(activated.astype(jnp.bfloat16), "dp", axis=0, tiled=False)
        all_hidden = lax.all_gather(hidden_grad, "dp", axis=0, tiled=False)

        partials = input_product(
            all_hidden.reshape(count, seg_rows, hidden), merged_up, n_dp, parts, segments
        )
        summed = lax.psum_scatter(
            partials.reshape(n_tensor, group_rows, width), "tensor",
            scatter_dimension=0, tiled=False,
        )
        input_grad = lax.ppermute(summed, both, returns)

        up_grad, inner_up = expert_grads(
            mix_grads, all_tokens, all_hidden[:, None], up_weight, segments
        )
        down_grad, inner_down = expert_grads(
            mix_grads, all_act[:, None], all_grads, down_weight, segments
        )
        inner = (inner_up + inner_down).reshape(count, sub, experts, sub)
        table = jnp.einsum("kaea->ke", inner).reshape(all_routes.shape)
        totals = lax.psum(table, both)
        route_grad = lax.dynamic_slice_in_dim(totals, lax.axis_index("dp"), 1, 0)
        return (input_grad, up_grad, down_grad, route_grad)

    return body


def solution(mesh):
    return jax.shard_map(
        make_body(mesh.shape["dp"], mesh.shape["tensor"]),
        mesh=mesh,
        in_specs=(
            P("dp", "tensor"),
            P("dp", "tensor"),
            P("dp", None, None),
            P("dp"),
            P(None, "dp", "tensor"),
            P(None, "tensor", "dp"),
        ),
        out_specs=(
            P("dp", "tensor"),
            P(None, "dp", "tensor"),
            P(None, "tensor", "dp"),
            P("dp", None, None),
        ),
        check_vma=False,
    )
```

time: 705 us -> 391 us (0.55); the launches traced: 695 us -> 389 us
  local copies, waits for them, and re-layouts: 224 us -> 14.6 us
  matrix products: 147 us -> 0 us
  Pallas kernels: 0 us -> 99.8 us
  waiting for transfers between devices: 224 us -> 147 us
  blocking collectives: 46.2 us -> 96 us
  starting transfers between devices: 22.9 us -> 11.3 us
  other arithmetic: 15.3 us -> 6.37 us
    all_to_all x4 -> x2, waiting for transfers between devices: 224 us -> 17.5 us  [the longest x1 17.5 us: body(): lax.all_to_all(back_parts.reshape(n_dp, group_rows, hidden), 'dp', 0, 0,...]
    dot_general x16 -> x0, matrix products: 147 us -> none  [the longest x1 25.5 us: body(): jnp.einsum('kdh,edh->ke', recv_up, up_weight, preferred_element_type=jnp....]
    pallas_call x0 -> x7, Pallas kernels: none -> 99.8 us  [the longest x2 36.6 us: expert_grads(): pl.pallas_call(lambda *refs: grad_kernel(segments, *refs), grid=(rows //...]
    unnamed x18 -> x19, local copies, waits for them, and re-layouts: 93.7 us -> 11.7 us
    all_gather x2 -> x4, waiting for transfers between devices: 0.01 us -> 80.4 us  [the longest x1 29.2 us: body(): all_grads = lax.all_gather(moved_grads, 'tensor', axis=0, tiled=False)]
    all_to_all x4 -> x0, local copies, waits for them, and re-layouts: 61 us -> none  [the longest x2 30.6 us: body(): lax.all_to_all(up_stack, 'dp', split_axis=1, concat_axis=0, tiled=True)]
    all_gather x1, blocking collectives: 6.28 us -> 54.6 us  [body(): all_routes = lax.all_gather(routes, 'dp', axis=0, tiled=True)]
    reduce_scatter x1, waiting for transfers between devices: 0.01 us -> 48.1 us  [body(): lax.psum_scatter(partials.reshape(n_tensor, group_rows, width), 'tensor',...]
  transfers between devices with their start and end apart: 7 -> 10, of which waited for: 4 -> 6; matrix products, arithmetic and copies ran while one was open for 45% -> 2% of each run, Pallas kernels for 0% -> 22%
where the time goes in v1:
time: 391 us; the launch traced here: 389 us
  waiting for transfers between devices  147 us (38%)
  Pallas kernels  99.8 us (26%)
  blocking collectives  96 us (25%)
  local copies, waits for them, and re-layouts  14.6 us (4%)
  between operations  14.6 us (4%)
  starting transfers between devices  11.3 us (3%)
  other arithmetic  6.37 us (2%)
    all_gather x1, blocking collectives, body(): all_routes = lax.all_gather(routes, 'dp', axis=0, tiled=True)  54.6 us
    reduce_scatter x1, waiting for transfers between devices, body(): lax.psum_scatter(partials.reshape(n_tensor, group_rows, width), 'tensor',...  48.1 us
    psum x1, blocking collectives, body(): totals = lax.psum(table, both)  41.4 us
    pallas_call x2, Pallas kernels, expert_grads(): pl.pallas_call(lambda *refs: grad_kernel(segments, *refs), grid=(rows //...  36.6 us
    all_gather x1, waiting for transfers between devices, body(): all_grads = lax.all_gather(moved_grads, 'tensor', axis=0, tiled=False)  29.2 us
    pallas_call x2, Pallas kernels, partial_product(): pl.pallas_call(lambda *refs: partial_kernel(turned, *refs), grid=(count,...  25.9 us
    pallas_call x2, Pallas kernels, merge(): pl.pallas_call(merge_kernel, grid=(rows // step,), in_specs=[pl.BlockSpec...  24.3 us
    all_gather x1, waiting for transfers between devices, body(): lax.all_gather(activated.astype(jnp.bfloat16), 'dp', axis=0, tiled=False)  21.4 us
  transfers between devices with their start and end apart: 10, of which 6 were waited for; matrix products, arithmetic and copies ran while one was open for 2% of the time, Pallas kernels for 22%

profile of v1, /device:TPU:0, one launch (start us, length us, event | category | flops | bytes accessed | tf_op | source)
XLA Modules:
  0.0 389.3 jit_solution(960771707464726791)
XLA Ops:
  7.2 0.0 all-gather.13.cloned.1.call-start
  7.2 1.6 collective-permute-start.1
  8.9 0.7 copy-done.7
  9.6 0.0 all-gather.13.cloned.1.call-update
  9.6 0.0 all-gather.11.cloned.1.call-start
  10.3 1.1 broadcast_select_fusion
  11.4 0.7 collective-permute-start
  12.1 0.7 copy-done.8
  12.9 54.6 %all_gather.25 = f32[4,2,16]{2,1,0:T(2,128)S(1)} all-gather(f32[1,2,16]{2,1,0:T(2,128)} %param.8), channel_id=1, replica_groups=mesh['dp'=4,'tensor'=8] {'dp'}, dimensions={0}, use_global_device_ids=true | all-gather | bytes 640 | tf_op jit(solution)/shard_map/all_gather | solution.py:241
  67.5 0.1 broadcast_multiply_fusion.1
  67.6 0.4 mul.221
  68.1 13.3 %merge.3.refs_1_.weight_ref = bf16[8,1024,512]{2,1,0:T(8,128)(2,1)} custom-call(bf16[256,256]{1,0:T(8,128)(2,1)S(1)} %pad_maximum_fusion.mix_ref, bf16[16,1024,512]{2,1,0:T(8,128)(2,1)} %refs_3_.2), custom_call_target="tpu_custom_call" | custom-call | flops 4294967296 | bytes 25165824 | tf_op jit(solution)/shard_map/merge/pallas_call | solution.py:44
  81.4 13.1 %all-gather.13.cloned.1.call-done = bf16[2816,512]{1,0:T(8,128)(2,1)} async-done(((bf16[352,512]{1,0:T(8,128)(2,1)}), bf16[2816,512]{1,0:T(8,128)(2,1)}) %all-gather.13.cloned.1.call-update) | async-done | bytes 2883600 | tf_op jit(solution)/shard_map/all_gather | solution.py:235
  94.5 1.8 copy-done
  96.3 12.7 %partial_product.3 = bf16[8,176,512]{2,1,0:T(8,128)(2,1)} custom-call(bf16[4,2,2,176,512]{4,3,2,1,0:T(8,128)(2,1)S(1)} %bitcast.35, bf16[8,1024,512]{2,1,0:T(8,128)(2,1)} %merge.3.refs_1_.weight_ref), custom_call_target="tpu_custom_call" | custom-call | flops 1476395008 | bytes 11272192 | tf_op jit(solution)/shard_map/partial_product/pallas_call | solution.py:90
  109.0 3.6 all-to-all-start.1
  112.5 11.1 %merge.2.refs_1_ = bf16[8,512,1024]{2,1,0:T(8,128)(2,1)} custom-call(bf16[256,256]{1,0:T(8,128)(2,1)S(1)} %pad_maximum_fusion.mix_ref, bf16[16,512,1024]{2,1,0:T(8,128)(2,1)} %refs_3_.3), custom_call_target="tpu_custom_call" | custom-call | flops 4294967296 | bytes 25165824 | tf_op jit(solution)/shard_map/merge/pallas_call | solution.py:44
  123.6 29.2 %all-gather.11.cloned.1.call-done = bf16[2816,512]{1,0:T(8,128)(2,1)} async-done(((bf16[352,512]{1,0:T(8,128)(2,1)}), bf16[2816,512]{1,0:T(8,128)(2,1)}) %all-gather.11.cloned.1.call-update) | async-done | bytes 2883600 | tf_op jit(solution)/shard_map/all_gather | solution.py:236
  152.8 1.8 copy-done.2
  154.6 13.2 %partial_product.2 = bf16[8,176,512]{2,1,0:T(8,128)(2,1)} custom-call(bf16[4,2,2,176,512]{4,3,2,1,0:T(8,128)(2,1)S(1)} %bitcast.37, bf16[8,512,1024]{2,1,0:T(8,128)(2,1)} %merge.2.refs_1_), custom_call_target="tpu_custom_call" | custom-call | flops 1476395008 | bytes 11272192 | tf_op jit(solution)/shard_map/partial_product/pallas_call | solution.py:90
  167.8 3.6 all-to-all-start
  171.3 0.0 all-gather.7.cloned.1.call-start
  171.4 1.1 convert_reduce_fusion
  172.4 17.5 %all-to-all-done = bf16[4,352,512]{2,1,0:T(8,128)(2,1)S(1)} async-done(((bf16[4,352,512]{2,1,0:T(8,128)(2,1)}), bf16[4,352,512]{2,1,0:T(8,128)(2,1)S(1)}, u32[]{:S(2)}, u32[]{:S(2)}) %all-to-all-start) | async-done | bytes 1441824 | tf_op jit(solution)/shard_map/all_to_all | solution.py:253
  190.0 0.2 convert_reduce_fusion.1
  190.2 2.5 multiply_convert_fusion
  192.7 0.0 reduce-scatter.2.cloned.1.call-start
  192.7 16.8 %all-gather.7.cloned.1.call-done = bf16[4,352,512]{2,1,0:T(8,128)(2,1)} async-done(((bf16[1,352,512]{2,1,0:T(8,128)(2,1)}), bf16[4,352,512]{2,1,0:T(8,128)(2,1)}) %all-gather.7.cloned.1.call-update) | async-done | bytes 1441808 | tf_op jit(solution)/shard_map/all_gather | solution.py:261
  209.5 1.4 copy-done.4
  210.8 13.0 %input_product.1 = bf16[4,2,2,176,512]{4,3,2,1,0:T(8,128)(2,1)} custom-call(bf16[8,176,512]{2,1,0:T(8,128)(2,1)S(1)} %bitcast.39, bf16[8,1024,512]{2,1,0:T(8,128)(2,1)} %merge.3.refs_1_.weight_ref), custom_call_target="tpu_custom_call" | custom-call | flops 1476395008 | bytes 11272192 | tf_op jit(solution)/shard_map/input_product/pallas_call | solution.py:123
  223.9 0.0 all-gather.9.cloned.1.call-start
  223.9 0.5 all-gather.9.cloned.1.call-update
  224.5 0.1 copy.12
  224.5 1.1 broadcast_multiply_fusion
  225.7 1.5 mul.240
  227.3 1.4 copy-done.5
  228.6 19.2 %expert_grads.2 = (bf16[16,1024,512]{2,1,0:T(8,128)(2,1)}, f32[128,256]{1,0:T(8,128)S(1)}) custom-call(bf16[256,256]{1,0:T(8,128)(2,1)S(1)} %pad_maximum_fusion.1.refs_0_, bf16[4,2,352,512]{3,2,1,0:T(8,128)(2,1)S(1)} %bitcast.36, bf16[4,1,352,512]{3,2,1,0:T(8,128)(2,1)S(1)} %bitcast.40, bf16[16,1024,512]{2,1,0:T(8,128)(2,1)} %refs_3_.2), custom_call_target="tpu_custom_call" | custom-call | flops 7918845952 | bytes 37879808 | tf_op jit(solution)/shard_map/expert_grads/pallas_call | solution.py:184
  247.8 48.1 %reduce-scatter.2.cloned.1.call-done = bf16[1,352,512]{2,1,0:T(8,128)(2,1)} async-done(((bf16[8,352,512]{2,1,0:T(8,128)(2,1)}), bf16[1,352,512]{2,1,0:T(8,128)(2,1)}) %reduce-scatter.2.cloned.1.call-update) | async-done | bytes 360464 | tf_op jit(solution)/shard_map/reduce_scatter | solution.py:266
  295.9 1.6 collective-permute-start.2
  297.5 21.4 %all-gather.9.cloned.1.call-done = bf16[4,352,512]{2,1,0:T(8,128)(2,1)} async-done(((bf16[1,352,512]{2,1,0:T(8,128)(2,1)}), bf16[4,352,512]{2,1,0:T(8,128)(2,1)}) %all-gather.9.cloned.1.call-update) | async-done | bytes 1441808 | tf_op jit(solution)/shard_map/all_gather | solution.py:260
  318.9 1.8 copy-done.3
  320.7 1.4 copy-done.6
  322.0 17.5 %expert_grads.3 = (bf16[16,512,1024]{2,1,0:T(8,128)(2,1)}, f32[128,256]{1,0:T(8,128)S(1)}) custom-call(bf16[256,256]{1,0:T(8,128)(2,1)S(1)} %pad_maximum_fusion.1.refs_0_, bf16[4,1,352,512]{3,2,1,0:T(8,128)(2,1)S(1)} %bitcast.41, bf16[4,2,352,512]{3,2,1,0:T(8,128)(2,1)S(1)} %bitcast.38, bf16[16,512,1024]{2,1,0:T(8,128)(2,1)} %refs_3_.3), custom_call_target="tpu_custom_call" | custom-call | flops 7918845952 | bytes 37879808 | tf_op jit(solution)/shard_map/expert_grads/pallas_call | solution.py:184
  339.5 0.3 reshape.142
  339.9 0.2 select_reduce_fusion
  340.0 41.4 %psum.7 = f32[4,2,16]{2,1,0:T(2,128)S(1)} all-reduce(f32[4,2,16]{2,1,0:T(2,128)S(1)} %bitcast.44), channel_id=1, replica_groups=mesh['dp'=4,'tensor'=8] {'dp','tensor'}, use_global_device_ids=true, to_apply=%region_4.5 | all-reduce | flops 128 | bytes 1024 | tf_op jit(solution)/shard_map/psum | solution.py:280
  381.4 0.6 constant_dynamic-slice_fusion
  382.0 0.7 copy.15
  (25 shorter events, 0.2 us)
Async XLA Ops:
  7.2 87.3 %all-gather.13.cloned.1.call-start = ((), (), s32[]{:S(2)}) async-start(), calls=%async_computation.7 | async-start | bytes 3244032 | tf_op jit(solution)/shard_map/all_gather | solution.py:235
  7.2 1.6 collective-permute-start.1
  8.9 0.7 copy-start.7
  9.6 143.1 %all-gather.11.cloned.1.call-start = ((), (), s32[]{:S(2)}) async-start(), calls=%async_computation.6 | async-start | bytes 3244032 | tf_op jit(solution)/shard_map/all_gather | solution.py:236
  11.4 0.7 collective-permute-start
  12.1 0.7 copy-start.8
  94.5 1.8 copy-start
  109.0 58.8 %all-to-all-start.1 = ((bf16[4,352,512]{2,1,0:T(8,128)(2,1)}), bf16[4,352,512]{2,1,0:T(8,128)(2,1)S(1)}, u32[]{:S(2)}, u32[]{:S(2)}) async-start(bf16[4,352,512]{2,1,0:T(8,128)(2,1)} %bitcast.6), calls=%async_computation.1 | async-start | bytes 2883584 | tf_op jit(solution)/shard_map/all_to_all | solution.py:249
  152.8 1.8 copy-start.2
  167.8 22.2 %all-to-all-start = ((bf16[4,352,512]{2,1,0:T(8,128)(2,1)}), bf16[4,352,512]{2,1,0:T(8,128)(2,1)S(1)}, u32[]{:S(2)}, u32[]{:S(2)}) async-start(bf16[4,352,512]{2,1,0:T(8,128)(2,1)} %bitcast.3), calls=%async_computation | async-start | bytes 2883584 | tf_op jit(solution)/shard_map/all_to_all | solution.py:253
  171.3 38.1 %all-gather.7.cloned.1.call-start = ((), (), s32[]{:S(2)}) async-start(), calls=%async_computation.3 | async-start | bytes 1802240 | tf_op jit(solution)/shard_map/all_gather | solution.py:261
  192.7 103.2 %reduce-scatter.2.cloned.1.call-start = ((), (), s32[]{:S(2)}) async-start(), calls=%async_computation.4 | async-start | bytes 3244032 | tf_op jit(solution)/shard_map/reduce_scatter | solution.py:266
  209.5 1.4 copy-start.4
  223.9 3.4 copy-start.1
  223.9 95.0 %all-gather.9.cloned.1.call-start = ((), (), s32[]{:S(2)}) async-start(), calls=%async_computation.5 | async-start | bytes 1802240 | tf_op jit(solution)/shard_map/all_gather | solution.py:260
  227.3 1.4 copy-start.5
  295.9 86.1 %collective-permute-start.2 = (bf16[352,512]{1,0:T(8,128)(2,1)}, bf16[352,512]{1,0:T(8,128)(2,1)S(1)}, u32[]{:S(2)}, u32[]{:S(2)}) collective-permute-start(bf16[352,512]{1,0:T(8,128)(2,1)} %bitcast.45), channel_id=1, source_target_pairs={{0,0},{1,1},{8,2},{9,3},{16,4},{17,5},{24,6},{25,7},{2,8},{3,9},{1... | collective-permute-start | bytes 1081352 | tf_op jit(solution)/shard_map/ppermute | solution.py:270
  318.9 1.8 copy-start.3
  320.7 1.4 copy-start.6
Sparse Core Ops, SparseCore 0:
  10.8 83.6 all-gather.12
  96.7 56.0 all-gather.10
  192.8 16.6 all-gather.6
  224.0 71.8 reduce-scatter.1
  297.9 20.9 all-gather.8

commit v2 on v1

--- a/solution.py
+++ b/solution.py
@@ -257,8 +257,9 @@
         back = jnp.sum(back_parts.astype(jnp.float32), axis=0)
         activated, slope = gelu_pair(pre)
         hidden_grad = (back * slope).astype(jnp.bfloat16)
-        all_act = lax.all_gather(activated.astype(jnp.bfloat16), "dp", axis=0, tiled=False)
-        all_hidden = lax.all_gather(hidden_grad, "dp", axis=0, tiled=False)
+        pair = jnp.stack([activated.astype(jnp.bfloat16), hidden_grad], axis=0)
+        all_pair = lax.all_gather(pair, "dp", axis=0, tiled=False)
+        all_act, all_hidden = all_pair[:, 0], all_pair[:, 1]
 
         partials = input_product(
             all_hidden.reshape(count, seg_rows, hidden), merged_up, n_dp, parts, segments

time: 391 us -> 377 us (0.964)
  waiting for transfers between devices: 147 us -> 133 us
    all_gather x2 -> x1, waiting for transfers between devices: 38.1 us -> 24.9 us  [body(): all_pair = lax.all_gather(pair, 'dp', axis=0, tiled=False)]
    unnamed x19 -> x13, local copies, waits for them, and re-layouts: 11.7 us -> 9.46 us
  transfers between devices with their start and end apart: 10 -> 9, of which waited for: 6 -> 5; matrix products, arithmetic and copies ran while one was open for 2% -> 2% of each run, Pallas kernels for 22% -> 23%
where the time goes in v2:
time: 377 us; the launch traced here: 375 us
  waiting for transfers between devices  133 us (35%)
  Pallas kernels  99.9 us (26%)
  blocking collectives  95.6 us (25%)
  between operations  14.6 us (4%)
  local copies, waits for them, and re-layouts  14.5 us (4%)
  starting transfers between devices  11.2 us (3%)
  other arithmetic  6.45 us (2%)
    all_gather x1, blocking collectives, body(): all_routes = lax.all_gather(routes, 'dp', axis=0, tiled=True)  54.6 us
    reduce_scatter x1, waiting for transfers between devices, body(): lax.psum_scatter(partials.reshape(n_tensor, group_rows, width), 'tensor',...  48.2 us
    psum x1, blocking collectives, body(): totals = lax.psum(table, both)  41 us
    pallas_call x2, Pallas kernels, expert_grads(): pl.pallas_call(lambda *refs: grad_kernel(segments, *refs), grid=(rows //...  36.6 us
    all_gather x1, waiting for transfers between devices, body(): all_grads = lax.all_gather(moved_grads, 'tensor', axis=0, tiled=False)  29.1 us
    pallas_call x2, Pallas kernels, partial_product(): pl.pallas_call(lambda *refs: partial_kernel(turned, *refs), grid=(count,...  25.9 us
    all_gather x1, waiting for transfers between devices, body(): all_pair = lax.all_gather(pair, 'dp', axis=0, tiled=False)  24.9 us
    pallas_call x2, Pallas kernels, merge(): pl.pallas_call(merge_kernel, grid=(rows // step,), in_specs=[pl.BlockSpec...  24.3 us
  transfers between devices with their start and end apart: 9, of which 5 were waited for; matrix products, arithmetic and copies ran while one was open for 2% of the time, Pallas kernels for 23%

profile of v2, /device:TPU:0, one launch (start us, length us, event | category | flops | bytes accessed | tf_op | source)
XLA Modules:
  0.0 375.1 jit_solution(15956409911127517989)
XLA Ops:
  7.2 0.0 all-gather.7.cloned.1.call-start
  7.2 1.6 collective-permute-start
  8.9 0.7 copy-done.4
  9.6 0.0 all-gather.7.cloned.1.call-update
  9.6 0.0 all-gather.9.cloned.1.call-start
  10.3 1.1 broadcast_select_fusion
  11.4 0.7 collective-permute-start.1
  12.1 0.7 copy-done.5
  12.9 0.0 all-gather.9.cloned.1.call-update
  12.9 54.6 %all_gather.23 = f32[4,2,16]{2,1,0:T(2,128)S(1)} all-gather(f32[1,2,16]{2,1,0:T(2,128)} %param.8), channel_id=1, replica_groups=mesh['dp'=4,'tensor'=8] {'dp'}, dimensions={0}, use_global_device_ids=true | all-gather | bytes 640 | tf_op jit(solution)/shard_map/all_gather | solution.py:241
  67.5 0.1 broadcast_multiply_fusion.1
  67.7 0.4 mul.221
  68.1 13.3 %merge.2.refs_1_.weight_ref = bf16[8,1024,512]{2,1,0:T(8,128)(2,1)} custom-call(bf16[256,256]{1,0:T(8,128)(2,1)S(1)} %pad_maximum_fusion.1.mix_ref, bf16[16,1024,512]{2,1,0:T(8,128)(2,1)} %refs_3_.2), custom_call_target="tpu_custom_call" | custom-call | flops 4294967296 | bytes 25165824 | tf_op jit(solution)/shard_map/merge/pallas_call | solution.py:44
  81.4 13.1 %all-gather.7.cloned.1.call-done = bf16[2816,512]{1,0:T(8,128)(2,1)} async-done(((bf16[352,512]{1,0:T(8,128)(2,1)}), bf16[2816,512]{1,0:T(8,128)(2,1)}) %all-gather.7.cloned.1.call-update) | async-done | bytes 2883600 | tf_op jit(solution)/shard_map/all_gather | solution.py:235
  94.5 1.8 copy-done
  96.3 12.7 %partial_product.2 = bf16[8,176,512]{2,1,0:T(8,128)(2,1)} custom-call(bf16[4,2,2,176,512]{4,3,2,1,0:T(8,128)(2,1)S(1)} %bitcast.35, bf16[8,1024,512]{2,1,0:T(8,128)(2,1)} %merge.2.refs_1_.weight_ref), custom_call_target="tpu_custom_call" | custom-call | flops 1476395008 | bytes 11272192 | tf_op jit(solution)/shard_map/partial_product/pallas_call | solution.py:90
  109.0 3.6 all-to-all-start
  112.6 11.1 %merge.3.refs_1_ = bf16[8,512,1024]{2,1,0:T(8,128)(2,1)} custom-call(bf16[256,256]{1,0:T(8,128)(2,1)S(1)} %pad_maximum_fusion.1.mix_ref, bf16[16,512,1024]{2,1,0:T(8,128)(2,1)} %refs_3_.3), custom_call_target="tpu_custom_call" | custom-call | flops 4294967296 | bytes 25165824 | tf_op jit(solution)/shard_map/merge/pallas_call | solution.py:44
  123.6 29.1 %all-gather.9.cloned.1.call-done = bf16[2816,512]{1,0:T(8,128)(2,1)} async-done(((bf16[352,512]{1,0:T(8,128)(2,1)}), bf16[2816,512]{1,0:T(8,128)(2,1)}) %all-gather.9.cloned.1.call-update) | async-done | bytes 2883600 | tf_op jit(solution)/shard_map/all_gather | solution.py:236
  152.8 1.8 copy-done.2
  154.6 13.2 %partial_product.3 = bf16[8,176,512]{2,1,0:T(8,128)(2,1)} custom-call(bf16[4,2,2,176,512]{4,3,2,1,0:T(8,128)(2,1)S(1)} %bitcast.37, bf16[8,512,1024]{2,1,0:T(8,128)(2,1)} %merge.3.refs_1_), custom_call_target="tpu_custom_call" | custom-call | flops 1476395008 | bytes 11272192 | tf_op jit(solution)/shard_map/partial_product/pallas_call | solution.py:90
  167.8 3.6 all-to-all-start.1
  171.3 0.0 all-gather.11.cloned.1.call-start
  171.4 1.1 convert_reduce_fusion.1
  172.4 17.5 %all-to-all-done.1 = bf16[4,352,512]{2,1,0:T(8,128)(2,1)S(1)} async-done(((bf16[4,352,512]{2,1,0:T(8,128)(2,1)}), bf16[4,352,512]{2,1,0:T(8,128)(2,1)S(1)}, u32[]{:S(2)}, u32[]{:S(2)}) %all-to-all-start.1) | async-done | bytes 1441824 | tf_op jit(solution)/shard_map/all_to_all | solution.py:253
  190.0 0.2 convert_reduce_fusion
  190.2 1.6 multiply_convert_fusion
  191.8 0.9 pad_maximum_fusion
  192.7 0.0 all-gather.11.cloned.1.call-update
  192.7 0.0 reduce-scatter.2.cloned.1.call-start
  192.8 24.9 %all-gather.11.cloned.1.call-done = bf16[8,352,512]{2,1,0:T(8,128)(2,1)} async-done(((bf16[2,352,512]{2,1,0:T(8,128)(2,1)}), bf16[8,352,512]{2,1,0:T(8,128)(2,1)}) %all-gather.11.cloned.1.call-update) | async-done | bytes 2883600 | tf_op jit(solution)/shard_map/all_gather | solution.py:261
  217.7 2.1 fusion.10
  219.8 13.1 %input_product.1 = bf16[4,2,2,176,512]{4,3,2,1,0:T(8,128)(2,1)} custom-call(bf16[8,176,512]{2,1,0:T(8,128)(2,1)S(1)} %bitcast.34, bf16[8,1024,512]{2,1,0:T(8,128)(2,1)} %merge.2.refs_1_.weight_ref), custom_call_target="tpu_custom_call" | custom-call | flops 1476395008 | bytes 11272192 | tf_op jit(solution)/shard_map/input_product/pallas_call | solution.py:123
  232.9 0.0 reduce-scatter.2.cloned.1.call-update
  232.9 0.1 copy.11
  233.0 1.1 broadcast_multiply_fusion
  234.1 1.5 mul.241
  235.7 1.8 copy-done.1
  237.5 19.2 %expert_grads.2 = (bf16[16,1024,512]{2,1,0:T(8,128)(2,1)}, f32[128,256]{1,0:T(8,128)S(1)}) custom-call(bf16[256,256]{1,0:T(8,128)(2,1)S(1)} %pad_maximum_fusion.2.refs_0_, bf16[4,2,352,512]{3,2,1,0:T(8,128)(2,1)S(1)} %bitcast.36, bf16[4,1,352,512]{3,2,1,0:T(8,128)(2,1)S(1)} %get-tuple-element.13.refs_2_, bf16[16,1024,512]{2,1,0:T(8,128)(2,1)} %refs_3_.2), custom_call_target="tpu_custom_call" | custom-call | flops 7918845952 | bytes 37879808 | tf_op jit(solution)/shard_map/expert_grads/pallas_call | solution.py:184
  256.7 48.2 %reduce-scatter.2.cloned.1.call-done = bf16[1,352,512]{2,1,0:T(8,128)(2,1)} async-done(((bf16[8,352,512]{2,1,0:T(8,128)(2,1)}), bf16[1,352,512]{2,1,0:T(8,128)(2,1)}) %reduce-scatter.2.cloned.1.call-update) | async-done | bytes 360464 | tf_op jit(solution)/shard_map/reduce_scatter | solution.py:267
  304.8 1.6 collective-permute-start.2
  306.5 1.8 copy-done.3
  308.3 17.5 %expert_grads.3 = (bf16[16,512,1024]{2,1,0:T(8,128)(2,1)}, f32[128,256]{1,0:T(8,128)S(1)}) custom-call(bf16[256,256]{1,0:T(8,128)(2,1)S(1)} %pad_maximum_fusion.2.refs_0_, bf16[4,1,352,512]{3,2,1,0:T(8,128)(2,1)S(1)} %get-tuple-element.12.refs_1_, bf16[4,2,352,512]{3,2,1,0:T(8,128)(2,1)S(1)} %bitcast.38, bf16[16,512,1024]{2,1,0:T(8,128)(2,1)} %refs_3_.3), custom_call_target="tpu_custom_call" | custom-call | flops 7918845952 | bytes 37879808 | tf_op jit(solution)/shard_map/expert_grads/pallas_call | solution.py:184
  325.8 0.3 reshape.138
  326.1 0.2 select_reduce_fusion
  326.3 41.0 %psum.7 = f32[4,2,16]{2,1,0:T(2,128)S(1)} all-reduce(f32[4,2,16]{2,1,0:T(2,128)S(1)} %bitcast.42), channel_id=1, replica_groups=mesh['dp'=4,'tensor'=8] {'dp','tensor'}, use_global_device_ids=true, to_apply=%region_4.5 | all-reduce | flops 128 | bytes 1024 | tf_op jit(solution)/shard_map/psum | solution.py:281
  367.2 0.6 constant_dynamic-slice_fusion
  367.8 0.7 copy.14
  (18 shorter events, 0.1 us)
Async XLA Ops:
  7.2 87.3 %all-gather.7.cloned.1.call-start = ((), (), s32[]{:S(2)}) async-start(), calls=%async_computation.4 | async-start | bytes 3244032 | tf_op jit(solution)/shard_map/all_gather | solution.py:235
  7.2 1.6 collective-permute-start
  8.9 0.7 copy-start.4
  9.6 143.1 %all-gather.9.cloned.1.call-start = ((), (), s32[]{:S(2)}) async-start(), calls=%async_computation.5 | async-start | bytes 3244032 | tf_op jit(solution)/shard_map/all_gather | solution.py:236
  11.4 0.7 collective-permute-start.1
  12.1 0.7 copy-start.5
  94.5 1.8 copy-start
  109.0 58.8 %all-to-all-start = ((bf16[4,352,512]{2,1,0:T(8,128)(2,1)}), bf16[4,352,512]{2,1,0:T(8,128)(2,1)S(1)}, u32[]{:S(2)}, u32[]{:S(2)}) async-start(bf16[4,352,512]{2,1,0:T(8,128)(2,1)} %bitcast.2), calls=%async_computation | async-start | bytes 2883584 | tf_op jit(solution)/shard_map/all_to_all | solution.py:249
  152.8 1.8 copy-start.2
  167.8 22.2 %all-to-all-start.1 = ((bf16[4,352,512]{2,1,0:T(8,128)(2,1)}), bf16[4,352,512]{2,1,0:T(8,128)(2,1)S(1)}, u32[]{:S(2)}, u32[]{:S(2)}) async-start(bf16[4,352,512]{2,1,0:T(8,128)(2,1)} %bitcast.6), calls=%async_computation.1 | async-start | bytes 2883584 | tf_op jit(solution)/shard_map/all_to_all | solution.py:253
  171.3 46.3 %all-gather.11.cloned.1.call-start = ((), (), s32[]{:S(2)}) async-start(), calls=%async_computation.6 | async-start | bytes 3604480 | tf_op jit(solution)/shard_map/all_gather | solution.py:261
  192.7 112.1 %reduce-scatter.2.cloned.1.call-start = ((), (), s32[]{:S(2)}) async-start(), calls=%async_computation.3 | async-start | bytes 3244032 | tf_op jit(solution)/shard_map/reduce_scatter | solution.py:267
  235.7 1.8 copy-start.1
  304.8 63.0 %collective-permute-start.2 = (bf16[352,512]{1,0:T(8,128)(2,1)}, bf16[352,512]{1,0:T(8,128)(2,1)S(1)}, u32[]{:S(2)}, u32[]{:S(2)}) collective-permute-start(bf16[352,512]{1,0:T(8,128)(2,1)} %bitcast.43), channel_id=1, source_target_pairs={{0,0},{1,1},{8,2},{9,3},{16,4},{17,5},{24,6},{25,7},{2,8},{3,9},{1... | collective-permute-start | bytes 1081352 | tf_op jit(solution)/shard_map/ppermute | solution.py:271
  306.5 1.8 copy-start.3
Sparse Core Ops, SparseCore 0:
  10.8 83.6 all-gather.6
  96.7 56.0 all-gather.8
  192.9 24.7 all-gather.10
  233.0 71.7 reduce-scatter.1
